TPU v7x, 512 devices: a whole 4x4x16 slice. The times are simulated.
512 devices in a mesh: gx: 16 (over z), gy: 4 (over x), gz: 8 (over y, core).
Axes of the slice: x: 4, y: 4, z: 16, core: 2. Of those that a mesh axis runs over, the one named last changes fastest.
Arguments:
- voxels: bfloat16 [128, 32, 32, 256], P('gx', 'gy', 'gz'), may hold values from -6 to 6
- conv_first: bfloat16 [27, 256, 256], P(None, None, 'gx'), may hold values from -0.078125 to 0.078125
- conv_second: bfloat16 [27, 256, 256], P(None, None, 'gx'), may hold values from -0.078125 to 0.078125
- head_weight: bfloat16 [256, 768], replicated, may hold values from -0.375 to 0.375
- teacher_in: bfloat16 [512, 768], P(None, 'gx'), may hold values from -0.25 to 0.25
- teacher_out: bfloat16 [768, 768], P(None, 'gx'), may hold values from -0.21875 to 0.21875
- tile_feats: bfloat16 [64, 256, 512], P('gx'), may hold values from -6 to 6
- interpolation: bfloat16 [8, 8, 8, 8, 256], replicated, may hold values from -0.125 to 0.125
- tile_lists: int32 [16, 4, 8, 8], P(None, 'gy', 'gz'), may hold values from 0 to 63, as said below
Outputs:
- prediction: bfloat16 [128, 32, 32, 768], P('gx', 'gy', 'gz')
- hidden_grad: bfloat16 [128, 32, 32, 256], P('gx', 'gy', 'gz')
Inputs may be any that keep to these rules, and one draw needn't show every extreme that they name: `tile_lists`: the 8 tiles of one brick lie in 8 different camera shards (tile t in shard t // 4); the two devices of one brick along gz (indices 2m and 2m+1) carry the same list.
All inputs are finite; a program needn't handle non-finite values.
Results may differ from a plain program's by a relative error of at most 0.0075.
Values may be sent and summed in bfloat16 or wider, within the bound.
A program may use at most 128 MiB of HBM per device.

v0:
```python
import jax
import jax.numpy as jnp
from jax import lax
from jax.sharding import PartitionSpec as P

offset_table = [
    (along_x, along_y, along_z)
    for along_x in range(3)
    for along_y in range(3)
    for along_z in range(3)
]


def with_halo(value, sides, width):
    for axis, dim in sides:
        count, length = (lax.axis_size(axis), value.shape[dim])
        up = [(i, (i + 1) % count) for i in range(count - 1)]
        down = [(j, i) for i, j in up]
        last = lax.slice_in_dim(value, length - width, length, axis=dim)
        leading = lax.slice_in_dim(value, 0, width, axis=dim)
        before = lax.ppermute(last, axis, up)
        after = lax.ppermute(leading, axis, down)
        value = jnp.concatenate([before, value, after], axis=dim)
    return value


def gather_patches(padded, count_x, count_y, count_z, flipped):
    pieces = []
    for along_x, along_y, along_z in offset_table:
        if flipped:
            corner = (2 - along_x, 2 - along_y, 2 - along_z, 0)
        else:
            corner = (along_x, along_y, along_z, 0)
        finish = (corner[0] + count_x, corner[1] + count_y, corner[2] + count_z, padded.shape[3])
        pieces.append(lax.slice(padded, corner, finish))
    return jnp.concatenate(pieces, axis=-1).reshape(count_x * count_y * count_z, -1)


def convolve_local(padded, matrix, counts, flipped):
    patches = gather_patches(padded, counts[0], counts[1], counts[2], flipped)
    product = jnp.dot(patches, matrix, preferred_element_type=jnp.float32)
    return product.reshape(counts[0], counts[1], counts[2], -1)


def teacher_features(source, first_weight, second_weight):
    count_tiles, pixels, channels = source.shape
    hidden_units = jax.nn.silu(
        jnp.dot(source.reshape(-1, channels), first_weight, preferred_element_type=jnp.float32)
    ).astype(jnp.bfloat16)
    values = jnp.dot(hidden_units, second_weight, preferred_element_type=jnp.float32)
    scaled = values * lax.rsqrt(jnp.mean(values * values, axis=-1, keepdims=True) + 1e-06)
    return scaled.astype(jnp.bfloat16).reshape(count_tiles, pixels, -1)


def silu_slope(pre_act):
    sigmoid = jax.nn.sigmoid(pre_act)
    return sigmoid * (1.0 + pre_act * (1.0 - sigmoid))


def local(
    voxels,
    conv_first,
    conv_second,
    head_weight,
    teacher_in,
    teacher_out,
    tile_feats,
    interpolation,
    tile_lists,
):
    first_full, second_full, teach_first, teach_second = (
        lax.all_gather(conv_first, "gx", axis=2, tiled=True),
        lax.all_gather(conv_second, "gx", axis=2, tiled=True),
        lax.all_gather(teacher_in, "gx", axis=1, tiled=True),
        lax.all_gather(teacher_out, "gx", axis=1, tiled=True),
    )
    size_x, size_y, size_z, channels = voxels.shape
    block = (size_x, size_y, size_z)
    first_matrix = first_full.reshape(-1, first_full.shape[2])
    second_matrix = second_full.reshape(-1, second_full.shape[2])
    flip_matrix = second_full.transpose(0, 2, 1).reshape(-1, second_full.shape[1])
    padded_in = with_halo(voxels, (("gx", 0), ("gy", 1), ("gz", 2)), 1)
    hidden = jax.nn.silu(convolve_local(padded_in, first_matrix, block, False)).astype(jnp.bfloat16)
    padded_hidden = with_halo(hidden, (("gx", 0), ("gy", 1), ("gz", 2)), 1)
    pre_second = convolve_local(padded_hidden, second_matrix, block, False)
    second_out = (hidden.astype(jnp.float32) + jax.nn.silu(pre_second)).astype(jnp.bfloat16)
    pred_full = jnp.dot(
        second_out.reshape(-1, channels), head_weight, preferred_element_type=jnp.float32
    )
    prediction = pred_full.astype(jnp.bfloat16).reshape(size_x, size_y, size_z, -1)
    line_lists = tile_lists.reshape(tile_lists.shape[0], tile_lists.shape[3])
    position = lax.axis_index("gx")
    per_shard = tile_feats.shape[0]
    owned_mask = line_lists // per_shard == position
    local_tile = jnp.sum(jnp.where(owned_mask, line_lists - position * per_shard, 0), axis=1)
    selector = (
        (local_tile[:, None] == jnp.arange(per_shard)[None, :])
        & jnp.any(owned_mask, axis=1)[:, None]
    ).astype(jnp.bfloat16)
    own_list = lax.dynamic_index_in_dim(line_lists, position, 0, keepdims=False)
    pick_table = (
        (own_list // per_shard)[:, None] == jnp.arange(line_lists.shape[0])[None, :]
    ).astype(jnp.bfloat16)
    source = teacher_features(tile_feats, teach_first, teach_second)
    outgoing = jnp.einsum(
        "dt,tpc->dpc", selector, source, preferred_element_type=jnp.float32
    ).astype(jnp.bfloat16)
    arrived = lax.all_to_all(outgoing, "gx", split_axis=0, concat_axis=0, tiled=True)
    features = jnp.einsum(
        "ks,spc->kpc", pick_table, arrived, preferred_element_type=jnp.float32
    ).astype(jnp.bfloat16)
    half_index = lax.axis_index("gz") % 2
    interp_rows = lax.dynamic_slice_in_dim(interpolation, half_index * size_z, size_z, 3)
    target = jnp.einsum(
        "kxyzp,kpd->xyzd", interp_rows, features, preferred_element_type=jnp.float32
    )
    residual_pred = (pred_full - target.reshape(-1, target.shape[3])).astype(jnp.bfloat16)
    grad_second = jnp.dot(residual_pred, head_weight.T, preferred_element_type=jnp.float32).reshape(
        size_x, size_y, size_z, -1
    )
    gate_grad = (grad_second * silu_slope(pre_second)).astype(jnp.bfloat16)
    padded_grad = with_halo(gate_grad, (("gx", 0), ("gy", 1), ("gz", 2)), 1)
    back_term = convolve_local(padded_grad, flip_matrix, block, True)
    hidden_grad = (grad_second + back_term).astype(jnp.bfloat16)
    return (prediction, hidden_grad)


def solution(mesh):
    in_specs = (
        P("gx", "gy", "gz", None),
        P(None, None, "gx"),
        P(None, None, "gx"),
        P(),
        P(None, "gx"),
        P(None, "gx"),
        P("gx", None, None),
        P(),
        P(None, "gy", "gz", None),
    )
    out_specs = (P("gx", "gy", "gz", None), P("gx", "gy", "gz", None))
    return jax.shard_map(local, mesh=mesh, in_specs=in_specs, out_specs=out_specs, check_vma=False)
```

profile of v0, /device:TPU:1, one launch (start us, length us, event | category | flops | bytes accessed | tf_op | source)
XLA Modules:
  0.0 561.5 jit_solution(4317218132013421539)
XLA Ops:
  9.3 35.7 %all_gather.14 = bf16[512,768]{0,1:T(8,128)(2,1)S(1)} all-gather(bf16[512,48]{0,1:T(8,128)(2,1)} %param.13), channel_id=1, replica_groups=mesh['gx'=16,'gy'=4,'gz'=8] {'gx'}, dimensions={1}, use_global_device_ids=true | all-gather | bytes 835584 | tf_op jit(solution)/shard_map/all_gather | solution.py:74
  45.0 32.6 %all-gather.8.cloned.1.call-done = bf16[768,768]{0,1:T(8,128)(2,1)} async-done(((bf16[768,48]{0,1:T(8,128)(2,1)}), bf16[768,768]{0,1:T(8,128)(2,1)}) %all-gather.8.cloned.1.call-update) | async-done | bytes 1179664 | tf_op jit(solution)/shard_map/all_gather | solution.py:75
  77.7 5.7 %multiply_reduce_fusion = (f32[1024]{0:T(1024)S(1)}, f32[1024,768]{1,0:T(8,128)}) fusion(bf16[768,768]{0,1:T(8,128)(2,1)} %all-gather.8.cloned.1.call-done, bf16[1024,512]{1,0:T(8,128)(2,1)} %bitcast.76, bf16[512,768]{0,1:T(8,128)(2,1)S(1)} %all_gather.14), kind=kOutput, calls=%fused_computation.7 | convolution fusion | flops 2018769920 | bytes 6164480 | tf_op jit(solution)/shard_map/dot_general | solution.py:50
  87.3 4.8 copy.64
  92.1 6.9 %all-to-all-start = ((bf16[16,256,768]{2,1,0:T(8,128)(2,1)}), bf16[16,256,768]{2,1,0:T(8,128)(2,1)}, u32[]{:S(2)}, u32[]{:S(2)}) async-start(bf16[16,256,768]{2,1,0:T(8,128)(2,1)} %copy.64), calls=%async_computation | async-start | bytes 12582912 | tf_op jit(solution)/shard_map/all_to_all | solution.py:108
  99.9 3.2 collective-permute-start
  104.4 274.9 %collective-permute-done = bf16[1,8,4,256]{3,1,2,0:T(8,128)(2,1)S(1)} collective-permute-done((bf16[1,8,4,256]{3,1,2,0:T(8,128)(2,1)S(1)}, bf16[1,8,4,256]{3,1,2,0:T(8,128)(2,1)S(1)}, u32[]{:S(2)}, u32[]{:S(2)}) %collective-permute-start) | collective-permute-done | bytes 16416 | tf_op jit(solution)/shard_map/ppermute | solution.py:21
  379.3 26.1 %collective-permute-done.1 = bf16[1,8,4,256]{3,1,2,0:T(8,128)(2,1)S(1)} collective-permute-done((bf16[1,8,4,256]{3,1,2,0:T(8,128)(2,1)S(1)}, bf16[1,8,4,256]{3,1,2,0:T(8,128)(2,1)S(1)}, u32[]{:S(2)}, u32[]{:S(2)}) %collective-permute-start.1) | collective-permute-done | bytes 16416 | tf_op jit(solution)/shard_map/ppermute | solution.py:22
  405.5 3.3 collective-permute-start.2
  410.1 3.8 collective-permute-done.3
  414.0 5.5 collective-permute-start.5
  443.6 5.7 %copy.28 = bf16[27,256,256]{2,1,0:T(8,128)(2,1)} copy(bf16[27,256,256]{1,2,0:T(8,128)(2,1)} %all-gather.4.cloned.1.call-done) | data formatting | bytes 7077888 | tf_op jit(solution)/shard_map/all_gather | solution.py:72
  449.3 4.2 multiply_convert_fusion.4
  453.5 3.2 collective-permute-start.6
  458.3 3.1 collective-permute-done.7
  461.4 3.4 collective-permute-start.8
  466.2 16.2 %all-gather.6.cloned.1.call-done = bf16[27,256,256]{1,2,0:T(8,128)(2,1)} async-done(((bf16[27,256,16]{1,2,0:T(8,128)(2,1)}), bf16[27,256,256]{1,2,0:T(8,128)(2,1)}) %all-gather.6.cloned.1.call-update) | async-done | bytes 3538960 | tf_op jit(solution)/shard_map/all_gather | solution.py:73
  482.4 5.7 %copy.29 = bf16[27,256,256]{2,1,0:T(8,128)(2,1)} copy(bf16[27,256,256]{1,2,0:T(8,128)(2,1)} %all-gather.6.cloned.1.call-done) | data formatting | bytes 7077888 | tf_op jit(solution)/shard_map/all_gather | solution.py:73
  488.2 10.8 %collective-permute-start.11 = (bf16[10,10,1,256]{3,1,2,0:T(8,128)(2,1)S(1)}, bf16[10,10,1,256]{3,1,2,0:T(8,128)(2,1)S(1)}, u32[]{:S(2)}, u32[]{:S(2)}) collective-permute-start(bf16[10,10,1,256]{3,1,2,0:T(8,128)(2,1)S(1)} %get-tuple-element.14), channel_id=1, source_target_pairs={{1,0},{2,1},{3,2},{4,3},{5,4},{6,5},{7,6},{9,8},{10,9},{11,10},{12... | collective-permute-start | bytes 153608 | tf_op jit(solution)/shard_map/ppermute | solution.py:22
  508.7 6.4 %fusion = bf16[8,256,768]{2,0,1:T(8,128)(2,1)S(1)} fusion(bf16[16,256,768]{2,1,0:T(8,128)(2,1)} %all-to-all-done, s32[8]{0:T(128)S(1)} %and_select_fusion), kind=kOutput, calls=%fused_computation.2 | convolution fusion | flops 50331776 | bytes 9437216 | tf_op jit(solution)/shard_map/ks,spc->kpc/dot_general | solution.py:109
  522.0 3.5 collective-permute-start.12
  526.8 3.2 collective-permute-done.13
  537.9 7.1 %collective-permute-start.17 = (bf16[10,10,1,256]{3,1,2,0:T(8,128)(2,1)S(1)}, bf16[10,10,1,256]{3,1,2,0:T(8,128)(2,1)S(1)}, u32[]{:S(2)}, u32[]{:S(2)}) collective-permute-start(bf16[10,10,1,256]{3,1,2,0:T(8,128)(2,1)S(1)} %get-tuple-element.10), channel_id=1, source_target_pairs={{0,1},{1,2},{2,3},{3,4},{4,5},{5,6},{6,7},{8,9},{9,10},{10,11},{11... | collective-permute-start | bytes 153608 | tf_op jit(solution)/shard_map/ppermute | solution.py:21
  547.4 3.4 collective-permute-done.16
  (160 shorter events, 68.5 us)
Async XLA Ops:
  7.2 507.9 %copy-start = (bf16[8,8,8,8,256]{4,3,2,1,0:T(8,128)(2,1)S(1)}, bf16[8,8,8,8,256]{4,3,2,1,0:T(8,128)(2,1)}, u32[]{:S(2)}) copy-start(bf16[8,8,8,8,256]{4,3,2,1,0:T(8,128)(2,1)} %param.16) | copy-start | bytes 6291460
  7.2 70.5 %all-gather.8.cloned.1.call-start = ((), (), s32[]{:S(2)}) async-start(), calls=%async_computation.3 | async-start | bytes 1253376 | tf_op jit(solution)/shard_map/all_gather | solution.py:75
  92.1 416.6 %all-to-all-start = ((bf16[16,256,768]{2,1,0:T(8,128)(2,1)}), bf16[16,256,768]{2,1,0:T(8,128)(2,1)}, u32[]{:S(2)}, u32[]{:S(2)}) async-start(bf16[16,256,768]{2,1,0:T(8,128)(2,1)} %copy.64), calls=%async_computation | async-start | bytes 12582912 | tf_op jit(solution)/shard_map/all_to_all | solution.py:108
  99.0 344.5 %all-gather.4.cloned.1.call-start = ((), (), s32[]{:S(2)}) async-start(), calls=%async_computation.1 | async-start | bytes 3760128 | tf_op jit(solution)/shard_map/all_gather | solution.py:72
  99.8 382.6 %all-gather.6.cloned.1.call-start = ((), (), s32[]{:S(2)}) async-start(), calls=%async_computation.2 | async-start | bytes 3760128 | tf_op jit(solution)/shard_map/all_gather | solution.py:73
  99.9 279.4 %collective-permute-start = (bf16[1,8,4,256]{3,1,2,0:T(8,128)(2,1)S(1)}, bf16[1,8,4,256]{3,1,2,0:T(8,128)(2,1)S(1)}, u32[]{:S(2)}, u32[]{:S(2)}) collective-permute-start(bf16[1,8,4,256]{3,1,2,0:T(8,128)(2,1)S(1)} %get-tuple-element.35), channel_id=1, source_target_pairs={{0,32},{32,64},{64,96},{96,128},{128,160},{160,192},{192,224},{224... | collective-permute-start | bytes 49160 | tf_op jit(solution)/shard_map/ppermute | solution.py:21
  103.1 302.3 %collective-permute-start.1 = (bf16[1,8,4,256]{3,1,2,0:T(8,128)(2,1)S(1)}, bf16[1,8,4,256]{3,1,2,0:T(8,128)(2,1)S(1)}, u32[]{:S(2)}, u32[]{:S(2)}) collective-permute-start(bf16[1,8,4,256]{3,1,2,0:T(8,128)(2,1)S(1)} %get-tuple-element.34), channel_id=1, source_target_pairs={{32,0},{64,32},{96,64},{128,96},{160,128},{192,160},{224,192},{256... | collective-permute-start | bytes 49160 | tf_op jit(solution)/shard_map/ppermute | solution.py:22
  405.5 4.6 collective-permute-start.2
  408.7 5.2 collective-permute-start.3
  414.0 8.5 %collective-permute-start.5 = (bf16[10,10,1,256]{3,1,2,0:T(8,128)(2,1)S(1)}, bf16[10,10,1,256]{3,1,2,0:T(8,128)(2,1)S(1)}, u32[]{:S(2)}, u32[]{:S(2)}) collective-permute-start(bf16[10,10,1,256]{3,1,2,0:T(8,128)(2,1)S(1)} %get-tuple-element.18), channel_id=1, source_target_pairs={{1,0},{2,1},{3,2},{4,3},{5,4},{6,5},{7,6},{9,8},{10,9},{11,10},{12... | collective-permute-start | bytes 153608 | tf_op jit(solution)/shard_map/ppermute | solution.py:22
  419.5 4.4 collective-permute-start.4
  449.3 8.7 %copy-start.5 = (s32[16,1,1,8]{0,3,2,1:T(8,128)S(1)}, s32[16,1,1,8]{0,3,2,1:T(8,128)}, u32[]{:S(2)}) copy-start(s32[16,1,1,8]{0,3,2,1:T(8,128)} %param.17) | copy-start | bytes 1540
  453.5 4.7 collective-permute-start.6
  456.8 4.6 collective-permute-start.7
  461.4 26.7 %collective-permute-start.8 = (bf16[10,1,4,256]{3,1,2,0:T(2,128)(2,1)S(1)}, bf16[10,1,4,256]{3,1,2,0:T(2,128)(2,1)S(1)}, u32[]{:S(2)}, u32[]{:S(2)}) collective-permute-start(bf16[10,1,4,256]{3,1,2,0:T(2,128)(2,1)S(1)} %get-tuple-element.26), channel_id=1, source_target_pairs={{0,8},{8,16},{16,24},{1,9},{9,17},{17,25},{2,10},{10,18},{18,26},{... | collective-permute-start | bytes 61448 | tf_op jit(solution)/shard_map/ppermute | solution.py:21
  464.8 23.3 %collective-permute-start.9 = (bf16[10,1,4,256]{3,1,2,0:T(2,128)(2,1)S(1)}, bf16[10,1,4,256]{3,1,2,0:T(2,128)(2,1)S(1)}, u32[]{:S(2)}, u32[]{:S(2)}) collective-permute-start(bf16[10,1,4,256]{3,1,2,0:T(2,128)(2,1)S(1)} %get-tuple-element.27), channel_id=1, source_target_pairs={{8,0},{16,8},{24,16},{9,1},{17,9},{25,17},{10,2},{18,10},{26,18},{... | collective-permute-start | bytes 61448 | tf_op jit(solution)/shard_map/ppermute | solution.py:22
  488.2 13.9 %collective-permute-start.11 = (bf16[10,10,1,256]{3,1,2,0:T(8,128)(2,1)S(1)}, bf16[10,10,1,256]{3,1,2,0:T(8,128)(2,1)S(1)}, u32[]{:S(2)}, u32[]{:S(2)}) collective-permute-start(bf16[10,10,1,256]{3,1,2,0:T(8,128)(2,1)S(1)} %get-tuple-element.14), channel_id=1, source_target_pairs={{1,0},{2,1},{3,2},{4,3},{5,4},{6,5},{7,6},{9,8},{10,9},{11,10},{12... | collective-permute-start | bytes 153608 | tf_op jit(solution)/shard_map/ppermute | solution.py:22
  499.0 4.3 collective-permute-start.10
  522.0 4.8 collective-permute-start.12
  525.5 4.5 collective-permute-start.13
  530.1 5.1 collective-permute-start.14
  533.1 4.7 collective-permute-start.15
  537.9 9.5 %collective-permute-start.17 = (bf16[10,10,1,256]{3,1,2,0:T(8,128)(2,1)S(1)}, bf16[10,10,1,256]{3,1,2,0:T(8,128)(2,1)S(1)}, u32[]{:S(2)}, u32[]{:S(2)}) collective-permute-start(bf16[10,10,1,256]{3,1,2,0:T(8,128)(2,1)S(1)} %get-tuple-element.10), channel_id=1, source_target_pairs={{0,1},{1,2},{2,3},{3,4},{4,5},{5,6},{6,7},{8,9},{9,10},{10,11},{11... | collective-permute-start | bytes 153608 | tf_op jit(solution)/shard_map/ppermute | solution.py:21
  545.1 5.8 %collective-permute-start.16 = (bf16[10,10,1,256]{3,1,2,0:T(8,128)(2,1)S(1)}, bf16[10,10,1,256]{3,1,2,0:T(8,128)(2,1)S(1)}, u32[]{:S(2)}, u32[]{:S(2)}) collective-permute-start(bf16[10,10,1,256]{3,1,2,0:T(8,128)(2,1)S(1)} %get-tuple-element.11), channel_id=1, source_target_pairs={{1,0},{2,1},{3,2},{4,3},{5,4},{6,5},{7,6},{9,8},{10,9},{11,10},{12... | collective-permute-start | bytes 153608 | tf_op jit(solution)/shard_map/ppermute | solution.py:22
  (4 other events, 13.6 us)
Sparse Core Ops, SparseCore 0:
  10.1 67.5 all-gather.7
  102.0 279.4 all-gather.3
  410.2 72.1 all-gather.5
where the time goes:
time: 563 us; the launch traced here: 562 us
  waiting for transfers between devices  370 us (66%)
  starting transfers between devices  65.7 us (12%)
  local copies, waits for them, and re-layouts  36.7 us (7%)
  blocking collectives  35.7 us (6%)
  matrix products  26.5 us (5%)
  between operations  14.6 us (3%)
  other arithmetic  12.5 us (2%)
    ppermute x9, waiting for transfers between devices, with_halo(): before = lax.ppermute(last, axis, up)  277 us
    ppermute x9, waiting for transfers between devices, with_halo(): after = lax.ppermute(leading, axis, down)  42.4 us
    all_gather x1, blocking collectives, local(): lax.all_gather(teacher_in, 'gx', axis=1, tiled=True)  35.7 us
    all_gather x1, waiting for transfers between devices, local(): lax.all_gather(teacher_out, 'gx', axis=1, tiled=True)  32.6 us
    ppermute x9, starting transfers between devices, with_halo(): before = lax.ppermute(last, axis, up)  32.6 us
    ppermute x9, starting transfers between devices, with_halo(): after = lax.ppermute(leading, axis, down)  26.1 us
    unnamed x82, local copies, waits for them, and re-layouts  17 us
    all_gather x1, waiting for transfers between devices, local(): lax.all_gather(conv_second, 'gx', axis=2, tiled=True)  16.2 us
  transfers between devices with their start and end apart: 22, of which 12 were waited for; matrix products, arithmetic and copies ran while one was open for 8% of the time, Pallas kernels for 0%

commit v1 on v0

v1 whole, which is shorter than its diff:
```python
import functools

import jax
import jax.numpy as jnp
import numpy as np
from jax import lax
from jax.experimental import pallas as pl
from jax.experimental.pallas import tpu as pltpu
from jax.sharding import PartitionSpec as P

MESH = pl.DeviceIdType.MESH
BF = jnp.bfloat16
F32 = jnp.float32
NT = (((1,), (1,)), ((), ()))

SECTIONS = (
    (0, -1, 0, 64),
    (0, 1, 64, 64),
    (-1, 0, 128, 32),
    (1, 0, 160, 32),
    (-1, -1, 192, 16),
    (-1, 1, 208, 16),
    (1, -1, 224, 16),
    (1, 1, 240, 16),
)


def source_row(x, y, z):
    dy = -1 if y < 0 else (1 if y > 7 else 0)
    dz = -1 if z < 0 else (1 if z > 3 else 0)
    if dy == 0 and dz == 0:
        return x * 32 + y * 4 + z
    for sy, sz, first, _ in SECTIONS:
        if (sy, sz) == (dy, dz):
            if dy == 0:
                return 256 + first + x * 8 + y
            if dz == 0:
                return 256 + first + x * 4 + z
            return 256 + first + x


def tables():
    shift = np.zeros((9, 256, 512), np.float32)
    for dy in range(3):
        for dz in range(3):
            for x in range(8):
                for y in range(8):
                    for z in range(4):
                        shift[dy * 3 + dz, x * 32 + y * 4 + z, source_row(x, y + dy - 1, z + dz - 1)] = 1
    stage = np.zeros((256, 256), np.float32)
    for sy, sz, first, _ in SECTIONS:
        ys = range(8) if sy == 0 else ([7] if sy < 0 else [0])
        zs = range(4) if sz == 0 else ([3] if sz < 0 else [0])
        for x in range(8):
            for y in ys:
                for z in zs:
                    if sy == 0:
                        row = first + x * 8 + y
                    elif sz == 0:
                        row = first + x * 4 + z
                    else:
                        row = first + x
                    stage[row, x * 32 + y * 4 + z] = 1
    plane = np.zeros((128, 512), np.float32)
    for side, x in ((0, 7), (1, 0)):
        for y in range(-1, 9):
            for z in range(-1, 5):
                plane[side * 64 + (y + 1) * 6 + z + 1, source_row(x, y, z)] = 1
    spread = np.zeros((288, 64), np.float32)
    for dy in range(3):
        for dz in range(3):
            for y in range(8):
                for z in range(4):
                    spread[(dy * 3 + dz) * 32 + y * 4 + z, (y + dy) * 6 + z + dz] = 1
    halves = np.zeros((512, 512), np.float32)
    for h in range(2):
        for uv in range(64):
            for w in range(4):
                halves[h * 256 + uv * 4 + w, uv * 8 + h * 4 + w] = 1
    return [jnp.asarray(t, BF) for t in (shift, stage, plane, spread, halves)]


def dot(a, b):
    return jnp.dot(a, b, preferred_element_type=F32)


def dot_nt(a, b):
    return lax.dot_general(a, b, NT, preferred_element_type=F32)


def kernel(
    blob, tiles, lists_in, voxels, head, interp, shift, stage, plane, spread, halves,
    pred_out, grad_out,
    G, R, A, B, F, IR, IP, FE, TS, TR, FA, S, SX, XR, P9, LV, LS, HP, ACC, PRE, GS, SO, PP,
    loc, zr, zs, ir, isn, sbs, sbr, l1s, l1r, l2s, l2r, a1s, a1r, a2s, a2r, hs, hr, xs, xr, ts, tr,
):
    gx, gy, gz = lax.axis_index("gx"), lax.axis_index("gy"), lax.axis_index("gz")
    cx, cy, core = gy, gz // 2, gz % 2
    sib = gz + 1 - 2 * core

    def chip(x, y, c):
        return (gx, x % 4, (y % 4) * 2 + c)

    def remote(src, dst, ss, rs, dev):
        return pltpu.make_async_remote_copy(
            src_ref=src, dst_ref=dst, send_sem=ss, recv_sem=rs, device_id=dev, device_id_type=MESH
        )

    def bytes_of(ref, sem):
        return pltpu.make_async_copy(ref, ref, sem)

    along = cy + core * (cx - cy)

    def weight_peer(k):
        return chip(cx + k * core, cy + k * (1 - core), core)

    first = cx + core * (cy - cx)
    second = cy + core * (cx - cy)

    def tile_peer(f, s, c):
        return chip(f + core * (s - f), s + core * (f - s), c)

    lanes = pl.ds(pl.multiple_of(core * 128, 128), 128)
    wide = pl.ds(pl.multiple_of(core * 256, 256), 256)
    quarter = pl.ds(along * 9, 9)

    def rows16(zb):
        return pl.ds(pl.multiple_of(zb * 16, 16), 16)

    barrier = pltpu.get_barrier_semaphore()
    partners = [((gx + 1) % 16, gy, gz), ((gx + 15) % 16, gy, gz)]
    partners += [(gx, (gy + k) % 4, gz) for k in (1, 2, 3)]
    partners += [(gx, gy, (gz + k) % 8) for k in range(1, 8)]
    partners += [(gx, (gy + i) % 4, (gz + j) % 8) for i in (1, 3) for j in (1, 7)]
    partners += [(gx, (gy + 2) % 4, sib)]
    for dev in partners:
        pl.semaphore_signal(barrier, inc=1, device_id=dev, device_id_type=MESH)

    own_w = pltpu.make_async_copy(
        blob.at[:, quarter, :, lanes], G.at[:, quarter, rows16(gx), lanes], loc.at[0]
    )
    own_w.start()
    pixels = pl.ds(pl.multiple_of((first * 4 + second) * 16, 16), 16)
    own_r = pltpu.make_async_copy(tiles.at[:, pixels, wide], R.at[pl.ds(gx * 4, 4)], loc.at[1])
    own_r.start()
    own_i = pltpu.make_async_copy(interp.at[pl.ds(core * 4, 4)], IR, loc.at[2])
    own_i.start()
    LV[cx, cy] = lists_in[...]

    def exists(dy, dz):
        y, z = gy + dy, gz + dz
        return (y >= 0) & (y < 4) & (z >= 0) & (z < 8)

    for dy, dz, at, rows in SECTIONS:

        @pl.when(jnp.logical_not(exists(dy, dz)))
        def _():
            for e in range(3):
                FA[e, 256 + at : 256 + at + rows] = jnp.zeros((rows, 256), BF)

    for side, there in ((0, gx > 0), (1, gx < 15)):

        @pl.when(jnp.logical_not(there))
        def _():
            for e in range(3):
                XR[e, side * 64 : side * 64 + 64] = jnp.zeros((64, 256), BF)

    def halo_copy(e, k):
        dy, dz, at, rows = SECTIONS[k]
        return remote(
            S.at[e, pl.ds(at, rows)], FA.at[e, pl.ds(256 + at, rows)], hs.at[e, k], hr.at[e, k],
            (gx, (gy - dy + 4) % 4, (gz - dz + 8) % 8),
        )

    def halo_stage(e, value):
        FA[e, 0:256] = value
        S[e] = dot(stage[...], value).astype(BF)

    def halo_send(e):
        for k, (dy, dz, _, _) in enumerate(SECTIONS):

            @pl.when(exists(-dy, -dz))
            def _():
                halo_copy(e, k).start()

    def plane_copy(e, side):
        return remote(
            SX.at[e, pl.ds(side * 64, 64)], XR.at[e, pl.ds(side * 64, 64)], xs.at[e, side], xr.at[e, side],
            ((gx + 1 - 2 * side + 16) % 16, gy, gz),
        )

    def halo_middle(e):
        for k, (dy, dz, _, _) in enumerate(SECTIONS):

            @pl.when(exists(dy, dz))
            def _():
                halo_copy(e, k).wait_recv()

            @pl.when(exists(-dy, -dz))
            def _():
                halo_copy(e, k).wait_send()

        SX[e] = dot(plane[...], FA[e]).astype(BF)
        for side, there in ((0, gx < 15), (1, gx > 0)):

            @pl.when(there)
            def _():
                plane_copy(e, side).start()

        def one(j, _):
            P9[j, 1:9] = dot(shift[j], FA[e]).astype(BF).reshape(8, 32, 256)
            return 0

        lax.fori_loop(0, 9, one, 0)

    def halo_end(e):
        for side in range(2):
            came = (gx > 0) if side == 0 else (gx < 15)
            went = (gx < 15) if side == 0 else (gx > 0)

            @pl.when(came)
            def _():
                plane_copy(e, side).wait_recv()

            @pl.when(went)
            def _():
                plane_copy(e, side).wait_send()

            spread_rows = dot(spread[...], XR[e, side * 64 : side * 64 + 64]).astype(BF)
            P9[:, 9 * side] = spread_rows.reshape(9, 32, 256)

    def block(i):
        return G[i // 36, i % 36]

    def convolve(base):
        ACC[...] = jnp.zeros_like(ACC)

        def one(j, _):
            total = ACC[...]
            for dx in range(3):
                total += dot_nt(P9[j, dx : dx + 8].reshape(256, 256), block(base + dx * 9 + j))
            ACC[...] = total
            return 0

        lax.fori_loop(0, 9, one, 0)

    def convolve_back(base):
        ACC[...] = jnp.zeros_like(ACC)

        def one(j, _):
            total = ACC[...]
            for dx in range(3):
                total += dot(P9[8 - j, 2 - dx : 10 - dx].reshape(256, 256), block(base + dx * 9 + j))
            ACC[...] = total
            return 0

        lax.fori_loop(0, 9, one, 0)

    halo_stage(0, voxels[...])
    own_w.wait()
    own_r.wait()
    pl.semaphore_wait(barrier, len(partners))

    def z_of(d, t):
        return (gx + 32 - t) % 16 if d == 0 else (gx + t) % 16

    def ring_copy(kind, d, t):
        zb = z_of(d, t)
        ref = R.at[pl.ds(zb * 4, 4)] if kind == 0 else G.at[kind - 1, quarter, rows16(zb), lanes]
        dev = ((gx + (1 if d == 0 else 15)) % 16, gy, gz)
        return remote(ref, ref, zs.at[kind], zr.at[kind, d, t + 1], dev)

    def ring_wait(kind, d, t):
        zb = z_of(d, t)
        ref = R.at[pl.ds(zb * 4, 4)] if kind == 0 else G.at[kind - 1, quarter, rows16(zb), lanes]
        bytes_of(ref, zr.at[kind, d, t]).wait()

    def piece(q, zb):
        return G.at[:, pl.ds((q % 4) * 9, 9), rows16(zb), lanes]

    def spread_copy(k, d, t):
        ref = piece(along, z_of(d, t))
        return remote(ref, ref, isn, ir.at[k - 1, d, t], weight_peer(k))

    def sibling_copy(q, d, t):
        ref = piece(q, z_of(d, t))
        return remote(ref, ref, sbs, sbr, (gx, gy, sib))

    def hand_out(d, t):
        for k in (1, 3, 2):
            spread_copy(k, d, t).start()
        sibling_copy(along, d, t).start()

    def take_in(d, t):
        for k in (1, 3, 2):
            bytes_of(piece(along + 4 - k, z_of(d, t)), ir.at[k - 1, d, t]).wait()
            sibling_copy(along + 4 - k, d, t).start()

    def list_first(k):
        return remote(lists_in, LV.at[cx, cy], l1s.at[k - 1], l1r.at[k - 1], (gx, (gy + k) % 4, gz))

    def list_second(k):
        ref = LV.at[:, cy]
        return remote(ref, ref, l2s.at[k - 1], l2r.at[k - 1], (gx, gy, (gz + 2 * k) % 8))

    for kind in range(3):
        for d in range(2):
            ring_copy(kind, d, 0).start()
    halo_send(0)
    for k in (1, 2, 3):
        list_first(k).start()
    hand_out(0, 0)

    def ring_step(t, _):
        for kind in range(3):
            for d in range(2):
                ring_wait(kind, d, t)
                if d == 0:
                    ring_copy(kind, d, t).start()
                else:

                    @pl.when(t < 7)
                    def _():
                        ring_copy(kind, d, t).start()

        for d in range(2):
            hand_out(d, t)

        @pl.when(t == 1)
        def _():
            take_in(0, 0)

        @pl.when(t > 1)
        def _():
            for d in range(2):
                take_in(d, t - 1)

        return 0

    lax.fori_loop(1, 3, ring_step, 0)
    for k in (1, 2, 3):
        bytes_of(LV.at[(cx + 4 - k) % 4, cy], l1r.at[k - 1]).wait()
        list_first(k).wait_send()
    for k in (1, 2, 3):
        list_second(k).start()
    halo_middle(0)
    column = lax.broadcasted_iota(jnp.int32, (768, 768), 1)
    natural = ((column & 255) >> 4) * 48 + (column >> 8) * 16 + (column & 15)
    order = (lax.broadcasted_iota(jnp.int32, (768, 768), 0) == natural).astype(BF)
    HP[...] = dot(head[...], order).astype(BF)
    lax.fori_loop(3, 5, ring_step, 0)
    halo_end(0)
    for k in (1, 2, 3):
        bytes_of(LV.at[:, (cy + 4 - k) % 4], l2r.at[k - 1]).wait()
        list_second(k).wait_send()
    to_smem = pltpu.make_async_copy(LV, LS, loc.at[3])
    to_smem.start()
    own_i.wait()

    def reorder(s, _):
        IP[s] = dot(halves[...], IR[s]).astype(BF)
        return 0

    lax.fori_loop(0, 4, reorder, 0)
    to_smem.wait()
    lax.fori_loop(5, 8, ring_step, 0)

    ring_wait(0, 0, 8)

    def first_copy(k):
        return remote(A.at[k - 1], B.at[:, :, first], a1s.at[k - 1], a1r.at[k - 1], tile_peer((first + k) % 4, second, core))

    def pick(k):
        f = (first + k) % 4

        def one(n, _):
            s = n // 8
            x = f + core * (s - f)
            y = s + core * (f - s)
            tile = R[LS[x, y, gx, n % 8]]
            if k == 0:
                B[s, n % 8, first] = tile
            else:
                A[k - 1, s, n % 8] = tile
            return 0

        lax.fori_loop(0, 32, one, 0)

    for k in (2, 1, 3):
        pick(k)
        first_copy(k).start()
    for kind in (1, 2):
        ring_wait(kind, 0, 8)
    hand_out(0, 8)
    for d in range(2):
        take_in(d, 7)
    pick(0)
    take_in(0, 8)
    half = G.at[:, :, :, lanes]
    other = G.at[:, :, :, pl.ds(pl.multiple_of((1 - core) * 128, 128), 128)]
    bytes_of(other, sbr).wait()

    convolve(0)
    pre = ACC[...]
    hidden = (pre * jax.nn.sigmoid(pre)).astype(BF)
    halo_stage(1, hidden)
    halo_send(1)

    for k in (1, 2, 3):
        bytes_of(B.at[:, :, (first + 4 - k) % 4], a1r.at[k - 1]).wait()

    def second_copy(k, flip):
        c = core + flip * (1 - 2 * core)
        s = (second + k) % 4
        return remote(
            B.at[s, pl.ds(c * 4, 4)], F.at[core, :, :, second], a2s.at[k, flip], a2r.at[k, flip], tile_peer(first, s, c)
        )

    stay = pltpu.make_async_copy(B.at[second, pl.ds(core * 4, 4)], F.at[core, :, :, second], loc.at[4])
    for k, flip in ((2, 0), (2, 1), (1, 0), (1, 1), (3, 0), (3, 1), (0, 1)):
        second_copy(k, flip).start()
    stay.start()

    halo_middle(1)
    halo_end(1)
    convolve(42)
    pre = ACC[...]
    PRE[...] = pre
    SO[...] = (FA[1, 0:256].astype(F32) + pre * jax.nn.sigmoid(pre)).astype(BF)

    def head_part(n, _):
        cols = pl.ds(pl.multiple_of(n * 256, 256), 256)
        pred_out[:, cols] = dot(SO[...], head[:, cols]).astype(BF)
        PP[:, cols] = dot(SO[...], HP[:, cols])
        return 0

    lax.fori_loop(0, 3, head_part, 0)

    stay.wait()
    bytes_of(F.at[core, :, :, 0], a2r.at[0, 1]).wait()
    for k in (1, 2, 3):
        for flip in range(2):
            bytes_of(F.at[core, :, :, 0], a2r.at[k, flip]).wait()

    def teach(s, _):
        left = F[0, s].reshape(256, 256)
        right = F[1, s].reshape(256, 256)
        units = []
        for a in range(3):
            raw = dot_nt(left, block(27 + 2 * a)) + dot_nt(right, block(28 + 2 * a))
            units.append((raw * jax.nn.sigmoid(raw)).astype(BF))
        values = []
        for a in range(3):
            part = dot_nt(units[0], block(33 + 3 * a))
            part += dot_nt(units[1], block(34 + 3 * a))
            part += dot_nt(units[2], block(35 + 3 * a))
            values.append(part)
        power = sum(jnp.sum(v * v, axis=1, keepdims=True) for v in values)
        scale = lax.rsqrt(power * (1.0 / 768.0) + 1e-6)
        for a in range(3):
            FE[s, :, a * 256 : (a + 1) * 256] = (values[a] * scale).astype(BF)
        return 0

    lax.fori_loop(0, 4, teach, 0)

    def target(h, into):
        rows = pl.ds(pl.multiple_of(h * 256, 256), 256)

        def one(n, _):
            cols = pl.ds(pl.multiple_of(n * 256, 256), 256)
            total = dot(IP[0, rows], FE[0, :, cols])
            for s in range(1, 4):
                total += dot(IP[s, rows], FE[s, :, cols])
            into(cols, total)
            return 0

        lax.fori_loop(0, 3, one, 0)

    def to_send(cols, total):
        TS[:, cols] = total

    def to_own(cols, total):
        PP[:, cols] = PP[:, cols] - total

    target(1 - core, to_send)
    swap = remote(TS, TR, ts, tr, (gx, gy, sib))
    swap.start()
    target(core, to_own)
    swap.wait()
    residual = (PP[...] - TR[...]).astype(BF)
    back = dot_nt(residual, HP[...])
    GS[...] = back
    pre = PRE[...]
    gate = jax.nn.sigmoid(pre)
    halo_stage(2, (back * (gate * (1.0 + pre * (1.0 - gate)))).astype(BF))
    halo_send(2)
    halo_middle(2)
    halo_end(2)
    convolve_back(42)
    grad_out[...] = (GS[...] + ACC[...]).astype(BF)

    bytes_of(R.at[pl.ds(0, 60)], zs.at[0]).wait()
    for kind in (1, 2):
        bytes_of(G.at[kind - 1, pl.ds(0, 9), pl.ds(0, 240), lanes], zs.at[kind]).wait()
    bytes_of(G.at[:, pl.ds(0, 27), :, lanes], isn).wait()
    bytes_of(half, sbs).wait()
    for k in (1, 2, 3):
        first_copy(k).wait_send()
    for k, flip in ((2, 0), (2, 1), (1, 0), (1, 1), (3, 0), (3, 1), (0, 1)):
        second_copy(k, flip).wait_send()


def local(voxels, conv_first, conv_second, head_weight, teacher_in, teacher_out, tile_feats, interpolation, tile_lists):
    first = conv_first.transpose(0, 2, 1)
    second = conv_second.transpose(0, 2, 1)
    t_in = teacher_in.reshape(2, 256, 3, 16).transpose(2, 0, 3, 1).reshape(6, 16, 256)
    t_out = teacher_out.reshape(16, 3, 16, 3, 16).transpose(3, 1, 4, 0, 2).reshape(9, 16, 256)
    blob = jnp.concatenate([first, t_in, t_out, second, jnp.zeros((3, 16, 256), BF)], axis=0)
    blob = blob.reshape(2, 36, 16, 256)
    lists = jnp.pad(tile_lists.reshape(16, 8), ((0, 0), (0, 120)))
    V = pltpu.VMEM
    D = pltpu.SemaphoreType.DMA
    scratch = [
        V((2, 36, 256, 256), BF),
        V((64, 16, 256), BF),
        V((3, 4, 8, 16, 256), BF),
        V((4, 8, 4, 16, 256), BF),
        V((2, 4, 4, 4, 16, 256), BF),
        V((4, 512, 256), BF),
        V((4, 512, 256), BF),
        V((4, 256, 768), BF),
        V((256, 768), F32),
        V((256, 768), F32),
        V((3, 512, 256), BF),
        V((3, 256, 256), BF),
        V((3, 128, 256), BF),
        V((3, 128, 256), BF),
        V((9, 10, 32, 256), BF),
        V((4, 4, 16, 128), jnp.int32),
        pltpu.SMEM((4, 4, 16, 128), jnp.int32),
        V((256, 768), BF),
        V((256, 256), F32),
        V((256, 256), F32),
        V((256, 256), F32),
        V((256, 256), BF),
        V((256, 768), F32),
        D((5,)),
        D((3, 2, 9)), D((3,)),
        D((3, 2, 9)), D,
        D, D,
        D((3,)), D((3,)), D((3,)), D((3,)),
        D((3,)), D((3,)), D((4, 2)), D((4, 2)),
        D((3, 8)), D((3, 8)), D((3, 2)), D((3, 2)),
        D, D,
    ]
    vm = pl.BlockSpec(memory_space=pltpu.VMEM)
    hbm = pl.BlockSpec(memory_space=pl.ANY)
    prediction, hidden_grad = pl.pallas_call(
        kernel,
        out_shape=(jax.ShapeDtypeStruct((256, 768), BF), jax.ShapeDtypeStruct((256, 256), BF)),
        in_specs=[hbm, hbm, vm, vm, vm, hbm, vm, vm, vm, vm, vm],
        out_specs=(vm, vm),
        scratch_shapes=scratch,
        compiler_params=pltpu.CompilerParams(
            collective_id=0, has_side_effects=True, vmem_limit_bytes=56 * 1024 * 1024
        ),
        cost_estimate=pl.CostEstimate(flops=6_000_000_000, bytes_accessed=10_000_000, transcendentals=1_000_000),
    )(
        blob, tile_feats, lists, voxels.reshape(256, 256), head_weight, interpolation.reshape(8, 512, 256), *tables()
    )
    return prediction.reshape(8, 8, 4, 768), hidden_grad.reshape(8, 8, 4, 256)


def solution(mesh):
    in_specs = (
        P("gx", "gy", "gz", None),
        P(None, None, "gx"),
        P(None, None, "gx"),
        P(),
        P(None, "gx"),
        P(None, "gx"),
        P("gx", None, None),
        P(),
        P(None, "gy", "gz", None),
    )
    out_specs = (P("gx", "gy", "gz", None), P("gx", "gy", "gz", None))
    return jax.shard_map(local, mesh=mesh, in_specs=in_specs, out_specs=out_specs, check_vma=False)
```

time: 563 us -> 102 us (0.18)
  waiting for transfers between devices: 370 us -> 0 us
  Pallas kernels: 0 us -> 93.9 us
  starting transfers between devices: 65.7 us -> 0 us
  blocking collectives: 35.7 us -> 0 us
  local copies, waits for them, and re-layouts: 36.7 us -> 7.51 us
  matrix products: 26.5 us -> 0 us
  between operations: 14.6 us -> 0.79 us
  other arithmetic: 12.5 us -> 0 us
    ppermute x18 -> x0, waiting for transfers between devices: 320 us -> none  [the longest x9 277 us: with_halo(): before = lax.ppermute(last, axis, up)]
    pallas_call x0 -> x1, Pallas kernels: none -> 93.9 us  [local(): pl.pallas_call(kernel, out_shape=(jax.ShapeDtypeStruct((256, 768), BF), j...]
    ppermute x18 -> x0, starting transfers between devices: 58.7 us -> none  [the longest x9 32.6 us: with_halo(): before = lax.ppermute(last, axis, up)]
    all_gather x3 -> x0, waiting for transfers between devices: 48.9 us -> none  [the longest x1 32.6 us: local(): lax.all_gather(teacher_out, 'gx', axis=1, tiled=True)]
    all_gather x1 -> x0, blocking collectives: 35.7 us -> none  [local(): lax.all_gather(teacher_in, 'gx', axis=1, tiled=True)]
    dot_general x9 -> x0, matrix products: 26.5 us -> none  [the longest x3 7.09 us: convolve_local(): product = jnp.dot(patches, matrix, preferred_element_type=jnp.float32)]
    unnamed x82 -> x16, local copies, waits for them, and re-layouts: 17 us -> 0.07 us
    all_gather x2 -> x0, local copies, waits for them, and re-layouts: 11.5 us -> none  [the longest x1 5.74 us: local(): lax.all_gather(conv_first, 'gx', axis=2, tiled=True)]
  transfers between devices with their start and end apart: 22 -> 0, of which waited for: 12 -> 0; matrix products, arithmetic and copies ran while one was open for 8% -> 0% of each run, Pallas kernels for 0% -> 0%
where the time goes in v1:
time: 102 us
  Pallas kernels  93.9 us (92%)
  local copies, waits for them, and re-layouts  7.51 us (7%)
    pallas_call x1, Pallas kernels, local(): pl.pallas_call(kernel, out_shape=(jax.ShapeDtypeStruct((256, 768), BF), j...  93.9 us
    reshape x2, local copies, waits for them, and re-layouts, local(): return (prediction.reshape(8, 8, 4, 768), hidden_grad.reshape(8, 8, 4, 256))  3.43 us
    reshape x2, local copies, waits for them, and re-layouts, local(): teacher_out.reshape(16, 3, 16, 3, 16).transpose(3, 1, 4, 0, 2)  2.45 us

profile of v1, /device:TPU:1, one launch (start us, length us, event | category | flops | bytes accessed | tf_op | source)
XLA Modules:
  0.0 102.2 jit_solution(16137681618391025689)
XLA Ops:
  0.6 0.0 copy-start
  0.6 0.0 copy-start.4
  0.7 0.0 copy-start.1
  0.7 0.0 copy-start.2
  0.7 0.0 copy-start.5
  0.7 1.9 %reshape.36 = bf16[16,3,16,3,16]{2,1,0,4,3:T(4,128)(2,1)S(1)} reshape(bf16[768,48]{0,1:T(8,128)(2,1)} %param.19) | data formatting | bytes 147456 | tf_op jit(solution)/shard_map/reshape | solution.py:517
  2.6 0.1 copy.22
  2.7 0.5 reshape.37
  3.2 0.0 copy-done
  3.3 0.0 copy-done.4
  3.3 0.0 copy-done.1
  3.4 0.0 copy-start.3
  3.4 0.0 copy-done.2
  3.4 0.8 reshape.40.voxels
  4.2 0.0 copy-done.5
  4.2 0.1 copy.23
  4.3 0.6 pad.4.lists_in
  4.9 0.0 copy-done.3
  4.9 93.9 %shard_map.149 = (bf16[256,768]{1,0:T(8,128)(2,1)}, bf16[256,256]{1,0:T(8,128)(2,1)}) custom-call(bf16[2,36,16,256]{3,2,1,0:T(8,128)(2,1)} %bitcast.19, bf16[4,256,512]{2,1,0:T(8,128)(2,1)} %tiles.1, s32[16,128]{1,0:T(8,128)} %pad.4.lists_in, bf16[256,256]{1,0:T(8,128)(2,1)} %reshape.40.voxels, bf16[256,768]{1,0:T(8,128)(2,1)} %head.1, ...), custom_call_target="tpu_custom_call" | custom-call | flops 6000000000 | bytes 10000000 | tf_op jit(solution)/shard_map/pallas_call | solution.py:558
  98.8 1.8 %reshape.42 = bf16[8,8,4,768]{3,2,1,0:T(4,128)(2,1)} reshape(bf16[256,768]{1,0:T(8,128)(2,1)} %get-tuple-element.4) | data formatting | bytes 786432 | tf_op jit(solution)/shard_map/reshape | solution.py:571
  100.6 1.6 %reshape.43 = bf16[8,8,4,256]{3,2,1,0:T(4,128)(2,1)} reshape(bf16[256,256]{1,0:T(8,128)(2,1)} %get-tuple-element.5) | data formatting | bytes 262144 | tf_op jit(solution)/shard_map/reshape | solution.py:571
  (7 shorter events, 0.1 us)
Async XLA Ops:
  0.6 2.6 %copy-start = (bf16[27,256,16]{1,2,0:T(8,128)(2,1)S(1)}, bf16[27,256,16]{1,2,0:T(8,128)(2,1)}, u32[]{:S(2)}) copy-start(bf16[27,256,16]{1,2,0:T(8,128)(2,1)} %param.15) | copy-start | bytes 663556
  0.6 2.6 %copy-start.4 = (bf16[512,48]{0,1:T(8,128)(2,1)S(1)}, bf16[512,48]{0,1:T(8,128)(2,1)}, u32[]{:S(2)}) copy-start(bf16[512,48]{0,1:T(8,128)(2,1)} %param.18) | copy-start | bytes 147460
  0.7 2.7 %copy-start.1 = (bf16[27,256,16]{1,2,0:T(8,128)(2,1)S(1)}, bf16[27,256,16]{1,2,0:T(8,128)(2,1)}, u32[]{:S(2)}) copy-start(bf16[27,256,16]{1,2,0:T(8,128)(2,1)} %param.16) | copy-start | bytes 663556
  0.7 2.7 %copy-start.2 = (bf16[8,8,4,256]{3,2,1,0:T(4,128)(2,1)S(1)}, bf16[8,8,4,256]{3,2,1,0:T(4,128)(2,1)}, u32[]{:S(2)}) copy-start(bf16[8,8,4,256]{3,2,1,0:T(4,128)(2,1)} %param.14) | copy-start | bytes 393220
  0.7 3.5 %copy-start.5 = (s32[16,1,1,8]{0,3,2,1:T(8,128)S(1)}, s32[16,1,1,8]{0,3,2,1:T(8,128)}, u32[]{:S(2)}) copy-start(s32[16,1,1,8]{0,3,2,1:T(8,128)} %param.22) | copy-start | bytes 1540
  3.4 1.5 %copy-start.3 = (bf16[72,16,256]{2,1,0:T(8,128)(2,1)}, bf16[72,16,256]{2,1,0:T(8,128)(2,1)S(1)}, u32[]{:S(2)}) copy-start(bf16[72,16,256]{2,1,0:T(8,128)(2,1)S(1)} %broadcast_dynamic-update-slice_fusion) | copy-start | bytes 1769476

commit v2 on v1

--- a/solution.py
+++ b/solution.py
@@ -122,13 +122,8 @@
 
     lanes = pl.ds(pl.multiple_of(core * 128, 128), 128)
     wide = pl.ds(pl.multiple_of(core * 256, 256), 256)
-    quarter = pl.ds(along * 9, 9)
-
-    def rows16(zb):
-        return pl.ds(pl.multiple_of(zb * 16, 16), 16)
-
     barrier = pltpu.get_barrier_semaphore()
-    partners = [((gx + 1) % 16, gy, gz), ((gx + 15) % 16, gy, gz)]
+    partners = [((gx + k) % 16, gy, gz) for k in (1, 15)]
     partners += [(gx, (gy + k) % 4, gz) for k in (1, 2, 3)]
     partners += [(gx, gy, (gz + k) % 8) for k in range(1, 8)]
     partners += [(gx, (gy + i) % 4, (gz + j) % 8) for i in (1, 3) for j in (1, 7)]
@@ -136,9 +131,7 @@
     for dev in partners:
         pl.semaphore_signal(barrier, inc=1, device_id=dev, device_id_type=MESH)
 
-    own_w = pltpu.make_async_copy(
-        blob.at[:, quarter, :, lanes], G.at[:, quarter, rows16(gx), lanes], loc.at[0]
-    )
+    own_w = pltpu.make_async_copy(blob.at[along, :, :, lanes], G.at[along, core, gx], loc.at[0])
     own_w.start()
     pixels = pl.ds(pl.multiple_of((first * 4 + second) * 16, 16), 16)
     own_r = pltpu.make_async_copy(tiles.at[:, pixels, wide], R.at[pl.ds(gx * 4, 4)], loc.at[1])
@@ -230,27 +223,37 @@
             P9[:, 9 * side] = spread_rows.reshape(9, 32, 256)
 
     def block(i):
-        return G[i // 36, i % 36]
-
-    def convolve(base):
+        parts = [G[i // 11, h, :, i % 11].reshape(256, 128) for h in range(2)]
+        return jnp.concatenate(parts, axis=1)
+
+    def block_second(i):
+        parts = [G[i // 7, h, :, 11 + i % 7].reshape(256, 128) for h in range(2)]
+        return jnp.concatenate(parts, axis=1)
+
+    def convolve_middle(blocks, back):
+        def one(j, total):
+            rows = P9[8 - j if back else j, 1:9].reshape(256, 256)
+            return total + (dot if back else dot_nt)(rows, blocks(9 + j))
+
         ACC[...] = jnp.zeros_like(ACC)
 
+        def three(i, _):
+            total = ACC[...]
+            for m in range(3):
+                total = one(3 * i + m, total)
+            ACC[...] = total
+            return 0
+
+        lax.fori_loop(0, 3, three, 0)
+
+    def convolve_sides(blocks, back):
         def one(j, _):
             total = ACC[...]
-            for dx in range(3):
-                total += dot_nt(P9[j, dx : dx + 8].reshape(256, 256), block(base + dx * 9 + j))
-            ACC[...] = total
-            return 0
-
-        lax.fori_loop(0, 9, one, 0)
-
-    def convolve_back(base):
-        ACC[...] = jnp.zeros_like(ACC)
-
-        def one(j, _):
-            total = ACC[...]
-            for dx in range(3):
-                total += dot(P9[8 - j, 2 - dx : 10 - dx].reshape(256, 256), block(base + dx * 9 + j))
+            for dx in (0, 2):
+                if back:
+                    total += dot(P9[8 - j, 2 - dx : 10 - dx].reshape(256, 256), blocks(dx * 9 + j))
+                else:
+                    total += dot_nt(P9[j, dx : dx + 8].reshape(256, 256), blocks(dx * 9 + j))
             ACC[...] = total
             return 0
 
@@ -264,37 +267,58 @@
     def z_of(d, t):
         return (gx + 32 - t) % 16 if d == 0 else (gx + t) % 16
 
+    limit = (8, 7)
+
+    def ring_piece(kind, d, t):
+        zb = z_of(d, t)
+        if kind == 0:
+            return R.at[pl.ds(zb * 4, 4)]
+        return G.at[along, core, zb, pl.ds(0, 11) if kind == 1 else pl.ds(11, 7)]
+
     def ring_copy(kind, d, t):
-        zb = z_of(d, t)
-        ref = R.at[pl.ds(zb * 4, 4)] if kind == 0 else G.at[kind - 1, quarter, rows16(zb), lanes]
+        ref = ring_piece(kind, d, t)
         dev = ((gx + (1 if d == 0 else 15)) % 16, gy, gz)
         return remote(ref, ref, zs.at[kind], zr.at[kind, d, t + 1], dev)
 
     def ring_wait(kind, d, t):
-        zb = z_of(d, t)
-        ref = R.at[pl.ds(zb * 4, 4)] if kind == 0 else G.at[kind - 1, quarter, rows16(zb), lanes]
-        bytes_of(ref, zr.at[kind, d, t]).wait()
-
-    def piece(q, zb):
-        return G.at[:, pl.ds((q % 4) * 9, 9), rows16(zb), lanes]
+        bytes_of(ring_piece(kind, d, t), zr.at[kind, d, t]).wait()
+
+    def piece(q, d, t):
+        return G.at[q % 4, core, z_of(d, t)]
 
     def spread_copy(k, d, t):
-        ref = piece(along, z_of(d, t))
+        ref = piece(along, d, t)
         return remote(ref, ref, isn, ir.at[k - 1, d, t], weight_peer(k))
 
     def sibling_copy(q, d, t):
-        ref = piece(q, z_of(d, t))
+        ref = piece(q, d, t)
         return remote(ref, ref, sbs, sbr, (gx, gy, sib))
 
     def hand_out(d, t):
-        for k in (1, 3, 2):
+        for k in (2, 1, 3):
             spread_copy(k, d, t).start()
         sibling_copy(along, d, t).start()
 
     def take_in(d, t):
         for k in (1, 3, 2):
-            bytes_of(piece(along + 4 - k, z_of(d, t)), ir.at[k - 1, d, t]).wait()
+            bytes_of(piece(along + 4 - k, d, t), ir.at[k - 1, d, t]).wait()
             sibling_copy(along + 4 - k, d, t).start()
+
+    def ring_step(t):
+        for kind in range(3):
+            for d in range(2):
+                if t <= limit[d]:
+                    ring_wait(kind, d, t)
+                if t < limit[d]:
+                    ring_copy(kind, d, t).start()
+        for d in range(2):
+            if t <= limit[d]:
+                hand_out(d, t)
+
+    def take_step(t):
+        for d in range(2):
+            if t <= limit[d] and (t > 0 or d == 0):
+                take_in(d, t)
 
     def list_first(k):
         return remote(lists_in, LV.at[cx, cy], l1s.at[k - 1], l1r.at[k - 1], (gx, (gy + k) % 4, gz))
@@ -303,58 +327,69 @@
         ref = LV.at[:, cy]
         return remote(ref, ref, l2s.at[k - 1], l2r.at[k - 1], (gx, gy, (gz + 2 * k) % 8))
 
+    def first_copy(k):
+        return remote(A.at[k - 1], B.at[:, :, first], a1s.at[k - 1], a1r.at[k - 1], tile_peer((first + k) % 4, second, core))
+
+    def pick(k):
+        f = (first + k) % 4
+
+        def one(s, _):
+            x = f + core * (s - f)
+            y = s + core * (f - s)
+            for n in range(8):
+                tile = R[LS[x, y, gx, n]]
+                if k == 0:
+                    B[s, n, first] = tile
+                else:
+                    A[k - 1, s, n] = tile
+            return 0
+
+        lax.fori_loop(0, 4, one, 0)
+
+    def second_copy(k, flip):
+        c = core + flip * (1 - 2 * core)
+        s = (second + k) % 4
+        return remote(
+            B.at[s, pl.ds(c * 4, 4)], F.at[core, :, :, second], a2s.at[k, flip], a2r.at[k, flip], tile_peer(first, s, c)
+        )
+
+    second_all = ((2, 0), (2, 1), (1, 0), (1, 1), (3, 0), (3, 1), (0, 1))
+
     for kind in range(3):
         for d in range(2):
             ring_copy(kind, d, 0).start()
-    halo_send(0)
     for k in (1, 2, 3):
         list_first(k).start()
+    halo_send(0)
     hand_out(0, 0)
 
-    def ring_step(t, _):
-        for kind in range(3):
-            for d in range(2):
-                ring_wait(kind, d, t)
-                if d == 0:
-                    ring_copy(kind, d, t).start()
-                else:
-
-                    @pl.when(t < 7)
-                    def _():
-                        ring_copy(kind, d, t).start()
-
-        for d in range(2):
-            hand_out(d, t)
-
-        @pl.when(t == 1)
-        def _():
-            take_in(0, 0)
-
-        @pl.when(t > 1)
-        def _():
-            for d in range(2):
-                take_in(d, t - 1)
-
-        return 0
-
-    lax.fori_loop(1, 3, ring_step, 0)
+    ring_step(1)
+    ring_step(2)
+    take_step(0)
     for k in (1, 2, 3):
         bytes_of(LV.at[(cx + 4 - k) % 4, cy], l1r.at[k - 1]).wait()
         list_first(k).wait_send()
     for k in (1, 2, 3):
         list_second(k).start()
+    ring_step(3)
+    take_step(1)
     halo_middle(0)
+    ring_step(4)
+    take_step(2)
     column = lax.broadcasted_iota(jnp.int32, (768, 768), 1)
     natural = ((column & 255) >> 4) * 48 + (column >> 8) * 16 + (column & 15)
     order = (lax.broadcasted_iota(jnp.int32, (768, 768), 0) == natural).astype(BF)
     HP[...] = dot(head[...], order).astype(BF)
-    lax.fori_loop(3, 5, ring_step, 0)
-    halo_end(0)
+    ring_step(5)
+    take_step(3)
     for k in (1, 2, 3):
         bytes_of(LV.at[:, (cy + 4 - k) % 4], l2r.at[k - 1]).wait()
         list_second(k).wait_send()
     to_smem = pltpu.make_async_copy(LV, LS, loc.at[3])
     to_smem.start()
+    halo_end(0)
+    ring_step(6)
+    take_step(4)
     own_i.wait()
 
     def reorder(s, _):
@@ -362,85 +397,39 @@
         return 0
 
     lax.fori_loop(0, 4, reorder, 0)
+    ring_step(7)
+    take_step(5)
     to_smem.wait()
-    lax.fori_loop(5, 8, ring_step, 0)
 
     ring_wait(0, 0, 8)
-
-    def first_copy(k):
-        return remote(A.at[k - 1], B.at[:, :, first], a1s.at[k - 1], a1r.at[k - 1], tile_peer((first + k) % 4, second, core))
-
-    def pick(k):
-        f = (first + k) % 4
-
-        def one(n, _):
-            s = n // 8
-            x = f + core * (s - f)
-            y = s + core * (f - s)
-            tile = R[LS[x, y, gx, n % 8]]
-            if k == 0:
-                B[s, n % 8, first] = tile
-            else:
-                A[k - 1, s, n % 8] = tile
-            return 0
-
-        lax.fori_loop(0, 32, one, 0)
-
     for k in (2, 1, 3):
         pick(k)
         first_copy(k).start()
     for kind in (1, 2):
         ring_wait(kind, 0, 8)
     hand_out(0, 8)
-    for d in range(2):
-        take_in(d, 7)
+    take_step(6)
     pick(0)
-    take_in(0, 8)
-    half = G.at[:, :, :, lanes]
-    other = G.at[:, :, :, pl.ds(pl.multiple_of((1 - core) * 128, 128), 128)]
-    bytes_of(other, sbr).wait()
-
-    convolve(0)
+    take_step(7)
+    take_step(8)
+    for k in (1, 2, 3):
+        bytes_of(B.at[:, :, (first + 4 - k) % 4], a1r.at[k - 1]).wait()
+    stay = pltpu.make_async_copy(B.at[second, pl.ds(core * 4, 4)], F.at[core, :, :, second], loc.at[4])
+    for k, flip in second_all:
+        second_copy(k, flip).start()
+    stay.start()
+    bytes_of(G.at[:, 1 - core], sbr).wait()
+
+    convolve_middle(block, False)
+    convolve_sides(block, False)
     pre = ACC[...]
     hidden = (pre * jax.nn.sigmoid(pre)).astype(BF)
     halo_stage(1, hidden)
     halo_send(1)
 
-    for k in (1, 2, 3):
-        bytes_of(B.at[:, :, (first + 4 - k) % 4], a1r.at[k - 1]).wait()
-
-    def second_copy(k, flip):
-        c = core + flip * (1 - 2 * core)
-        s = (second + k) % 4
-        return remote(
-            B.at[s, pl.ds(c * 4, 4)], F.at[core, :, :, second], a2s.at[k, flip], a2r.at[k, flip], tile_peer(first, s, c)
-        )
-
-    stay = pltpu.make_async_copy(B.at[second, pl.ds(core * 4, 4)], F.at[core, :, :, second], loc.at[4])
-    for k, flip in ((2, 0), (2, 1), (1, 0), (1, 1), (3, 0), (3, 1), (0, 1)):
-        second_copy(k, flip).start()
-    stay.start()
-
-    halo_middle(1)
-    halo_end(1)
-    convolve(42)
-    pre = ACC[...]
-    PRE[...] = pre
-    SO[...] = (FA[1, 0:256].astype(F32) + pre * jax.nn.sigmoid(pre)).astype(BF)
-
-    def head_part(n, _):
-        cols = pl.ds(pl.multiple_of(n * 256, 256), 256)
-        pred_out[:, cols] = dot(SO[...], head[:, cols]).astype(BF)
-        PP[:, cols] = dot(SO[...], HP[:, cols])
-        return 0
-
-    lax.fori_loop(0, 3, head_part, 0)
-
     stay.wait()
-    bytes_of(F.at[core, :, :, 0], a2r.at[0, 1]).wait()
-    for k in (1, 2, 3):
-        for flip in range(2):
-            bytes_of(F.at[core, :, :, 0], a2r.at[k, flip]).wait()
+    for k, flip in second_all:
+        bytes_of(F.at[core, :, :, 0], a2r.at[k, flip]).wait()
 
     def teach(s, _):
         left = F[0, s].reshape(256, 256)
@@ -461,8 +450,6 @@
             FE[s, :, a * 256 : (a + 1) * 256] = (values[a] * scale).astype(BF)
         return 0
 
-    lax.fori_loop(0, 4, teach, 0)
-
     def target(h, into):
         rows = pl.ds(pl.multiple_of(h * 256, 256), 256)
 
@@ -471,42 +458,61 @@
             total = dot(IP[0, rows], FE[0, :, cols])
             for s in range(1, 4):
                 total += dot(IP[s, rows], FE[s, :, cols])
-            into(cols, total)
+            into[:, cols] = total
             return 0
 
         lax.fori_loop(0, 3, one, 0)
 
-    def to_send(cols, total):
-        TS[:, cols] = total
-
-    def to_own(cols, total):
-        PP[:, cols] = PP[:, cols] - total
-
-    target(1 - core, to_send)
+    lax.fori_loop(0, 1, teach, 0)
+    halo_middle(1)
+    lax.fori_loop(1, 3, teach, 0)
+    halo_end(1)
+    lax.fori_loop(3, 4, teach, 0)
+    target(1 - core, TS)
     swap = remote(TS, TR, ts, tr, (gx, gy, sib))
     swap.start()
-    target(core, to_own)
+    target(core, PP)
+
+    convolve_middle(block_second, False)
+    convolve_sides(block_second, False)
+    pre = ACC[...]
+    PRE[...] = pre
+    SO[...] = (FA[1, 0:256].astype(F32) + pre * jax.nn.sigmoid(pre)).astype(BF)
     swap.wait()
-    residual = (PP[...] - TR[...]).astype(BF)
-    back = dot_nt(residual, HP[...])
+
+    def head_part(n, _):
+        cols = pl.ds(pl.multiple_of(n * 256, 256), 256)
+        PP[:, cols] = dot(SO[...], HP[:, cols]) - (PP[:, cols] + TR[:, cols])
+        return 0
+
+    lax.fori_loop(0, 3, head_part, 0)
+    back = dot_nt(PP[...].astype(BF), HP[...])
     GS[...] = back
     pre = PRE[...]
     gate = jax.nn.sigmoid(pre)
     halo_stage(2, (back * (gate * (1.0 + pre * (1.0 - gate)))).astype(BF))
     halo_send(2)
+
+    def predict(n, _):
+        cols = pl.ds(pl.multiple_of(n * 256, 256), 256)
+        pred_out[:, cols] = dot(SO[...], head[:, cols]).astype(BF)
+        return 0
+
+    lax.fori_loop(0, 3, predict, 0)
     halo_middle(2)
+    convolve_middle(block_second, True)
     halo_end(2)
-    convolve_back(42)
+    convolve_sides(block_second, True)
     grad_out[...] = (GS[...] + ACC[...]).astype(BF)
 
     bytes_of(R.at[pl.ds(0, 60)], zs.at[0]).wait()
-    for kind in (1, 2):
-        bytes_of(G.at[kind - 1, pl.ds(0, 9), pl.ds(0, 240), lanes], zs.at[kind]).wait()
-    bytes_of(G.at[:, pl.ds(0, 27), :, lanes], isn).wait()
-    bytes_of(half, sbs).wait()
+    bytes_of(G.at[along, core, pl.ds(0, 15), pl.ds(0, 11)], zs.at[1]).wait()
+    bytes_of(G.at[along, core, pl.ds(0, 15), pl.ds(11, 7)], zs.at[2]).wait()
+    bytes_of(G.at[pl.ds(0, 3), core], isn).wait()
+    bytes_of(G.at[:, core], sbs).wait()
     for k in (1, 2, 3):
         first_copy(k).wait_send()
-    for k, flip in ((2, 0), (2, 1), (1, 0), (1, 1), (3, 0), (3, 1), (0, 1)):
+    for k, flip in second_all:
         second_copy(k, flip).wait_send()
 
 
@@ -515,13 +521,14 @@
     second = conv_second.transpose(0, 2, 1)
     t_in = teacher_in.reshape(2, 256, 3, 16).transpose(2, 0, 3, 1).reshape(6, 16, 256)
     t_out = teacher_out.reshape(16, 3, 16, 3, 16).transpose(3, 1, 4, 0, 2).reshape(9, 16, 256)
-    blob = jnp.concatenate([first, t_in, t_out, second, jnp.zeros((3, 16, 256), BF)], axis=0)
-    blob = blob.reshape(2, 36, 16, 256)
+    early = jnp.concatenate([first, t_in, t_out, jnp.zeros((2, 16, 256), BF)], axis=0).reshape(4, 11, 16, 256)
+    late = jnp.concatenate([second, jnp.zeros((1, 16, 256), BF)], axis=0).reshape(4, 7, 16, 256)
+    blob = jnp.concatenate([early, late], axis=1)
     lists = jnp.pad(tile_lists.reshape(16, 8), ((0, 0), (0, 120)))
     V = pltpu.VMEM
     D = pltpu.SemaphoreType.DMA
     scratch = [
-        V((2, 36, 256, 256), BF),
+        V((4, 2, 16, 18, 16, 128), BF),
         V((64, 16, 256), BF),
         V((3, 4, 8, 16, 256), BF),
         V((4, 8, 4, 16, 256), BF),

time: 102 us -> 95.8 us (0.939)
  Pallas kernels: 93.9 us -> 86.4 us
    pallas_call x1, Pallas kernels: 93.9 us -> 86.4 us  [local(): pl.pallas_call(kernel, out_shape=(jax.ShapeDtypeStruct((256, 768), BF), j...]
where the time goes in v2:
time: 95.8 us; the launch traced here: 95.6 us
  Pallas kernels  86.4 us (90%)
  local copies, waits for them, and re-layouts  7.46 us (8%)
  other arithmetic  0.99 us (1%)
    pallas_call x1, Pallas kernels, local(): pl.pallas_call(kernel, out_shape=(jax.ShapeDtypeStruct((256, 768), BF), j...  86.4 us
    reshape x2, local copies, waits for them, and re-layouts, local(): return (prediction.reshape(8, 8, 4, 768), hidden_grad.reshape(8, 8, 4, 256))  3.43 us
    reshape x2, local copies, waits for them, and re-layouts, local(): teacher_out.reshape(16, 3, 16, 3, 16).transpose(3, 1, 4, 0, 2)  2.42 us

profile of v2, /device:TPU:1, one launch (start us, length us, event | category | flops | bytes accessed | tf_op | source)
XLA Modules:
  0.0 95.6 jit_solution(15945352861755585229)
XLA Ops:
  0.6 0.0 copy-start.3
  0.6 0.0 copy-start
  0.7 0.0 copy-start.1
  0.7 1.9 %reshape.39 = bf16[16,3,16,3,16]{2,1,0,4,3:T(4,128)(2,1)S(1)} reshape(bf16[768,48]{0,1:T(8,128)(2,1)} %param.19) | data formatting | bytes 147456 | tf_op jit(solution)/shard_map/reshape | solution.py:523
  2.6 0.0 copy-start.2
  2.6 0.0 copy-start.4
  2.6 0.1 copy.22
  2.7 0.5 reshape.40
  3.2 0.0 copy-done.3
  3.3 0.1 pad.11.clone
  3.3 0.0 copy-done
  3.4 0.1 maximum_maximum_fusion
  3.5 0.0 copy-done.1
  3.5 0.9 pad_maximum_fusion.blob
  4.4 0.0 copy-done.2
  4.4 0.7 reshape.44.voxels
  5.1 0.0 copy-done.4
  5.1 0.1 copy.23
  5.2 0.6 pad.5.lists_in
  5.8 86.4 %shard_map.149 = (bf16[256,768]{1,0:T(8,128)(2,1)}, bf16[256,256]{1,0:T(8,128)(2,1)}) custom-call(bf16[4,18,16,256]{3,2,1,0:T(8,128)(2,1)} %pad_maximum_fusion.blob, bf16[4,256,512]{2,1,0:T(8,128)(2,1)} %tiles.1, s32[16,128]{1,0:T(8,128)} %pad.5.lists_in, bf16[256,256]{1,0:T(8,128)(2,1)} %reshape.44.voxels, bf16[256,768]{1,0:T(8,128)(2,1)} %head.1, ...), custom_call_target="tpu_custom_call" | custom-call | flops 6000000000 | bytes 10000000 | tf_op jit(solution)/shard_map/pallas_call | solution.py:565
  92.1 1.8 %reshape.46 = bf16[8,8,4,768]{3,2,1,0:T(4,128)(2,1)} reshape(bf16[256,768]{1,0:T(8,128)(2,1)} %get-tuple-element.4) | data formatting | bytes 786432 | tf_op jit(solution)/shard_map/reshape | solution.py:578
  94.0 1.6 %reshape.47 = bf16[8,8,4,256]{3,2,1,0:T(4,128)(2,1)} reshape(bf16[256,256]{1,0:T(8,128)(2,1)} %get-tuple-element.5) | data formatting | bytes 262144 | tf_op jit(solution)/shard_map/reshape | solution.py:578
  (4 shorter events, 0.0 us)
Async XLA Ops:
  0.6 2.6 %copy-start.3 = (bf16[512,48]{0,1:T(8,128)(2,1)S(1)}, bf16[512,48]{0,1:T(8,128)(2,1)}, u32[]{:S(2)}) copy-start(bf16[512,48]{0,1:T(8,128)(2,1)} %param.18) | copy-start | bytes 147460
  0.6 2.7 %copy-start = (bf16[27,256,16]{1,2,0:T(8,128)(2,1)S(1)}, bf16[27,256,16]{1,2,0:T(8,128)(2,1)}, u32[]{:S(2)}) copy-start(bf16[27,256,16]{1,2,0:T(8,128)(2,1)} %param.15) | copy-start | bytes 663556
  0.7 2.8 %copy-start.1 = (bf16[27,256,16]{1,2,0:T(8,128)(2,1)S(1)}, bf16[27,256,16]{1,2,0:T(8,128)(2,1)}, u32[]{:S(2)}) copy-start(bf16[27,256,16]{1,2,0:T(8,128)(2,1)} %param.16) | copy-start | bytes 663556
  2.6 1.8 %copy-start.2 = (bf16[8,8,4,256]{3,2,1,0:T(4,128)(2,1)S(1)}, bf16[8,8,4,256]{3,2,1,0:T(4,128)(2,1)}, u32[]{:S(2)}) copy-start(bf16[8,8,4,256]{3,2,1,0:T(4,128)(2,1)} %param.14) | copy-start | bytes 393220
  2.6 2.5 %copy-start.4 = (s32[16,1,1,8]{0,3,2,1:T(8,128)S(1)}, s32[16,1,1,8]{0,3,2,1:T(8,128)}, u32[]{:S(2)}) copy-start(s32[16,1,1,8]{0,3,2,1:T(8,128)} %param.22) | copy-start | bytes 1540

commit v3 on v2

--- a/solution.py
+++ b/solution.py
@@ -89,9 +89,9 @@
 
 
 def kernel(
-    blob, tiles, lists_in, voxels, head, interp, shift, stage, plane, spread, halves,
+    blob, tiles, lists_in, voxels, head, interp, shift_in, stage, plane, spread, halves_in,
     pred_out, grad_out,
-    G, R, A, B, F, IR, IP, FE, TS, TR, FA, S, SX, XR, P9, LV, LS, HP, ACC, PRE, GS, SO, PP,
+    shift, halves, G, R, A, B, F, IR, IP, FE, TS, TR, FA, S, SX, XR, P9, LV, LS, HP, ACC, PRE, GS, SO, PP,
     loc, zr, zs, ir, isn, sbs, sbr, l1s, l1r, l2s, l2r, a1s, a1r, a2s, a2r, hs, hr, xs, xr, ts, tr,
 ):
     gx, gy, gz = lax.axis_index("gx"), lax.axis_index("gy"), lax.axis_index("gz")
@@ -138,6 +138,10 @@
     own_r.start()
     own_i = pltpu.make_async_copy(interp.at[pl.ds(core * 4, 4)], IR, loc.at[2])
     own_i.start()
+    own_s = pltpu.make_async_copy(shift_in, shift, loc.at[5])
+    own_s.start()
+    own_h = pltpu.make_async_copy(halves_in, halves, loc.at[6])
+    own_h.start()
     LV[cx, cy] = lists_in[...]
 
     def exists(dy, dz):
@@ -346,12 +350,17 @@
 
         lax.fori_loop(0, 4, one, 0)
 
-    def second_copy(k, flip):
+    def second_copy(k, flip, m):
         c = core + flip * (1 - 2 * core)
-        s = (second + k) % 4
+        s, f = (second + k) % 4, (first + 4 - m) % 4
         return remote(
-            B.at[s, pl.ds(c * 4, 4)], F.at[core, :, :, second], a2s.at[k, flip], a2r.at[k, flip], tile_peer(first, s, c)
+            B.at[s, pl.ds(c * 4, 4), f], F.at[core, :, f, second], a2s.at[k, flip, m], a2r.at[k, flip, m],
+            tile_peer(first, s, c),
         )
+
+    def second_send(m):
+        for k, flip in second_all:
+            second_copy(k, flip, m).start()
 
     second_all = ((2, 0), (2, 1), (1, 0), (1, 1), (3, 0), (3, 1), (0, 1))
 
@@ -373,6 +382,7 @@
         list_second(k).start()
     ring_step(3)
     take_step(1)
+    own_s.wait()
     halo_middle(0)
     ring_step(4)
     take_step(2)
@@ -391,6 +401,7 @@
     ring_step(6)
     take_step(4)
     own_i.wait()
+    own_h.wait()
 
     def reorder(s, _):
         IP[s] = dot(halves[...], IR[s]).astype(BF)
@@ -408,15 +419,17 @@
     for kind in (1, 2):
         ring_wait(kind, 0, 8)
     hand_out(0, 8)
+    pick(0)
+    second_send(0)
     take_step(6)
-    pick(0)
+    for k in (1, 3):
+        bytes_of(B.at[:, :, (first + 4 - k) % 4], a1r.at[k - 1]).wait()
+        second_send(k)
     take_step(7)
+    bytes_of(B.at[:, :, (first + 2) % 4], a1r.at[1]).wait()
+    second_send(2)
     take_step(8)
-    for k in (1, 2, 3):
-        bytes_of(B.at[:, :, (first + 4 - k) % 4], a1r.at[k - 1]).wait()
     stay = pltpu.make_async_copy(B.at[second, pl.ds(core * 4, 4)], F.at[core, :, :, second], loc.at[4])
-    for k, flip in second_all:
-        second_copy(k, flip).start()
     stay.start()
     bytes_of(G.at[:, 1 - core], sbr).wait()
 
@@ -429,7 +442,8 @@
 
     stay.wait()
     for k, flip in second_all:
-        bytes_of(F.at[core, :, :, 0], a2r.at[k, flip]).wait()
+        for m in range(4):
+            bytes_of(F.at[core, :, 0, 0], a2r.at[k, flip, m]).wait()
 
     def teach(s, _):
         left = F[0, s].reshape(256, 256)
@@ -513,14 +527,19 @@
     for k in (1, 2, 3):
         first_copy(k).wait_send()
     for k, flip in second_all:
-        second_copy(k, flip).wait_send()
+        for m in range(4):
+            second_copy(k, flip, m).wait_send()
 
 
 def local(voxels, conv_first, conv_second, head_weight, teacher_in, teacher_out, tile_feats, interpolation, tile_lists):
     first = conv_first.transpose(0, 2, 1)
     second = conv_second.transpose(0, 2, 1)
-    t_in = teacher_in.reshape(2, 256, 3, 16).transpose(2, 0, 3, 1).reshape(6, 16, 256)
-    t_out = teacher_out.reshape(16, 3, 16, 3, 16).transpose(3, 1, 4, 0, 2).reshape(9, 16, 256)
+    t_in = teacher_in.T.reshape(3, 16, 2, 256).transpose(0, 2, 1, 3).reshape(6, 16, 256)
+    unit = np.arange(768)
+    order = np.zeros((768, 768), np.float32)
+    order[(unit % 256) // 16 * 48 + unit // 256 * 16 + unit % 16, unit] = 1
+    t_out = dot(teacher_out.T, jnp.asarray(order, BF)).astype(BF)
+    t_out = t_out.reshape(3, 16, 3, 256).transpose(0, 2, 1, 3).reshape(9, 16, 256)
     early = jnp.concatenate([first, t_in, t_out, jnp.zeros((2, 16, 256), BF)], axis=0).reshape(4, 11, 16, 256)
     late = jnp.concatenate([second, jnp.zeros((1, 16, 256), BF)], axis=0).reshape(4, 7, 16, 256)
     blob = jnp.concatenate([early, late], axis=1)
@@ -528,6 +547,7 @@
     V = pltpu.VMEM
     D = pltpu.SemaphoreType.DMA
     scratch = [
+        V((9, 256, 512), BF), V((512, 512), BF),
         V((4, 2, 16, 18, 16, 128), BF),
         V((64, 16, 256), BF),
         V((3, 4, 8, 16, 256), BF),
@@ -551,12 +571,12 @@
         V((256, 256), F32),
         V((256, 256), BF),
         V((256, 768), F32),
-        D((5,)),
+        D((7,)),
         D((3, 2, 9)), D((3,)),
         D((3, 2, 9)), D,
         D, D,
         D((3,)), D((3,)), D((3,)), D((3,)),
-        D((3,)), D((3,)), D((4, 2)), D((4, 2)),
+        D((3,)), D((3,)), D((4, 2, 4)), D((4, 2, 4)),
         D((3, 8)), D((3, 8)), D((3, 2)), D((3, 2)),
         D, D,
     ]
@@ -565,7 +585,7 @@
     prediction, hidden_grad = pl.pallas_call(
         kernel,
         out_shape=(jax.ShapeDtypeStruct((256, 768), BF), jax.ShapeDtypeStruct((256, 256), BF)),
-        in_specs=[hbm, hbm, vm, vm, vm, hbm, vm, vm, vm, vm, vm],
+        in_specs=[hbm, hbm, vm, vm, vm, hbm, hbm, vm, vm, vm, hbm],
         out_specs=(vm, vm),
         scratch_shapes=scratch,
         compiler_params=pltpu.CompilerParams(

time: 95.8 us -> 95.7 us (level)
  local copies, waits for them, and re-layouts: 7.46 us -> 5.85 us
  matrix products: 0 us -> 1.6 us
    reshape x3 -> x2, local copies, waits for them, and re-layouts: 2.44 us -> 0.06 us  [the longest x1 0.04 us: local(): t_out.reshape(3, 16, 3, 256).transpose(0, 2, 1, 3).reshape(9, 16, 256)]
    dot_general x0 -> x1, matrix products: none -> 1.6 us  [dot(): return jnp.dot(a, b, preferred_element_type=F32)]
where the time goes in v3:
time: 95.7 us; the launch traced here: 95.4 us
  Pallas kernels  86.2 us (90%)
  local copies, waits for them, and re-layouts  5.85 us (6%)
  matrix products  1.6 us (2%)
  other arithmetic  0.99 us (1%)
    pallas_call x1, Pallas kernels, local(): pl.pallas_call(kernel, out_shape=(jax.ShapeDtypeStruct((256, 768), BF), j...  86.2 us
    reshape x2, local copies, waits for them, and re-layouts, local(): return (prediction.reshape(8, 8, 4, 768), hidden_grad.reshape(8, 8, 4, 256))  3.43 us

profile of v3, /device:TPU:1, one launch (start us, length us, event | category | flops | bytes accessed | tf_op | source)
XLA Modules:
  0.0 95.4 jit_solution(6156698439472311258)
XLA Ops:
  0.6 0.0 copy-start
  0.6 0.0 copy-start.4
  0.7 0.0 copy-start.1
  0.7 0.0 copy-start.2
  0.7 0.8 copy-done
  1.5 1.6 %fusion = bf16[48,768]{1,0:T(8,128)(2,1)S(1)} fusion(bf16[768,48]{0,1:T(8,128)(2,1)S(1)} %copy-done, bf16[768,768]{1,0:T(8,128)(2,1)} %constant.7.clone), kind=kOutput, calls=%fused_computation.1 | convolution fusion | flops 56659968 | bytes 1327104 | tf_op jit(solution)/shard_map/dot_general | solution.py:84
  3.2 0.0 copy-done.4
  3.2 0.0 copy-start.3
  3.3 0.1 pad.11.clone
  3.3 0.0 copy-done.1
  3.3 0.0 copy-start.5
  3.3 0.1 maximum_maximum_fusion
  3.5 0.0 copy-done.2
  3.5 0.9 pad_maximum_fusion.blob
  4.4 0.0 copy-done.3
  4.4 0.7 reshape.44.voxels
  5.1 0.0 copy-done.5
  5.1 0.1 copy.24
  5.1 0.6 pad.5.lists_in
  5.7 86.2 %shard_map.158 = (bf16[256,768]{1,0:T(8,128)(2,1)}, bf16[256,256]{1,0:T(8,128)(2,1)}) custom-call(bf16[4,18,16,256]{3,2,1,0:T(8,128)(2,1)} %pad_maximum_fusion.blob, bf16[4,256,512]{2,1,0:T(8,128)(2,1)} %tiles.1, s32[16,128]{1,0:T(8,128)} %pad.5.lists_in, bf16[256,256]{1,0:T(8,128)(2,1)} %reshape.44.voxels, bf16[256,768]{1,0:T(8,128)(2,1)} %head.1, ...), custom_call_target="tpu_custom_call" | custom-call | flops 6000000000 | bytes 10000000 | tf_op jit(solution)/shard_map/pallas_call | solution.py:585
  92.0 1.8 %reshape.46 = bf16[8,8,4,768]{3,2,1,0:T(4,128)(2,1)} reshape(bf16[256,768]{1,0:T(8,128)(2,1)} %get-tuple-element.4) | data formatting | bytes 786432 | tf_op jit(solution)/shard_map/reshape | solution.py:598
  93.8 1.6 %reshape.47 = bf16[8,8,4,256]{3,2,1,0:T(4,128)(2,1)} reshape(bf16[256,256]{1,0:T(8,128)(2,1)} %get-tuple-element.5) | data formatting | bytes 262144 | tf_op jit(solution)/shard_map/reshape | solution.py:598
  (6 shorter events, 0.1 us)
Async XLA Ops:
  0.6 0.9 copy-start
  0.6 2.5 %copy-start.4 = (bf16[512,48]{0,1:T(8,128)(2,1)S(1)}, bf16[512,48]{0,1:T(8,128)(2,1)}, u32[]{:S(2)}) copy-start(bf16[512,48]{0,1:T(8,128)(2,1)} %param.19) | copy-start | bytes 147460
  0.7 2.7 %copy-start.1 = (bf16[27,256,16]{1,2,0:T(8,128)(2,1)S(1)}, bf16[27,256,16]{1,2,0:T(8,128)(2,1)}, u32[]{:S(2)}) copy-start(bf16[27,256,16]{1,2,0:T(8,128)(2,1)} %param.16) | copy-start | bytes 663556
  0.7 2.8 %copy-start.2 = (bf16[27,256,16]{1,2,0:T(8,128)(2,1)S(1)}, bf16[27,256,16]{1,2,0:T(8,128)(2,1)}, u32[]{:S(2)}) copy-start(bf16[27,256,16]{1,2,0:T(8,128)(2,1)} %param.17) | copy-start | bytes 663556
  3.2 1.1 %copy-start.3 = (bf16[8,8,4,256]{3,2,1,0:T(4,128)(2,1)S(1)}, bf16[8,8,4,256]{3,2,1,0:T(4,128)(2,1)}, u32[]{:S(2)}) copy-start(bf16[8,8,4,256]{3,2,1,0:T(4,128)(2,1)} %param.15) | copy-start | bytes 393220
  3.3 1.7 %copy-start.5 = (s32[16,1,1,8]{0,3,2,1:T(8,128)S(1)}, s32[16,1,1,8]{0,3,2,1:T(8,128)}, u32[]{:S(2)}) copy-start(s32[16,1,1,8]{0,3,2,1:T(8,128)} %param.23) | copy-start | bytes 1540
